TPU v7x, 256 devices: a whole 4x4x8 slice. The times are simulated.
256 devices in a mesh: leaf: 256 (over z, x, y, core).
Axes of the slice: x: 4, y: 4, z: 8, core: 2. Of those that a mesh axis runs over, the one named last changes fastest.
Arguments:
- densities: float32 [16, 524288], P(None, 'leaf'), may hold values from -6 to 6
- panels: float32 [3, 524288], P(None, 'leaf'), may hold values from -4 to 4
- areas: float32 [524288], P('leaf'), may hold values from 0.1 to 1
- near_offsets: int32 [8192, 6], P('leaf'), may hold values from -4 to 4, as said below
- near_count: int32 [8192], P('leaf'), may hold values from 1 to 6, as said below
- leaf_basis: float32 [8192, 64, 64], P('leaf'), may hold values from -0.25 to 0.25
- local_trans: float32 [15872, 64, 64], P('leaf'), may hold values from -0.625 to 0.625
- local_coupling: float32 [15872, 64, 64], P('leaf'), may hold values from -0.75 to 0.75
- up_trans: float32 [256, 8, 64, 64], P('leaf'), as said below
- coupling: float32 [256, 8, 64, 64], P('leaf'), as said below
Outputs:
- potential: float32 [16, 524288], P(None, 'leaf')
Inputs may be any that keep to these rules, and one draw needn't show every extreme that they name: `near_offsets`: each row lists distinct offsets, the first is 0 (the leaf itself). Only the first near_count slots of a leaf's list are used; the first leaf of every device uses all 6. `up_trans`: entries are equal on all devices of one level-k cluster. `coupling`: entries are equal on all devices of one level-k cluster.
All inputs are finite; a program needn't handle non-finite values.
Results may differ from a plain program's by a relative error of at most 0.0003.
Values sent between devices are 32-bit elements; how exact they have to be, the bound alone decides.
A program may use at most 128 MiB of HBM per device.

v0:
```python
import jax
import jax.numpy as jnp
from jax import lax
from jax.sharding import PartitionSpec as P

LEAF = 64
RANK = 64
RHS = 16
HALO_LEAVES = 4
NNEAR = 6


softening = 0.25
highest = lax.Precision.HIGHEST


def with_halo(block, sides, width):
    for axis, dim in sides:
        count = lax.axis_size(axis)
        forward = [(i, i + 1) for i in range(count - 1)]
        backward = [(target, source) for source, target in forward]
        low = lax.ppermute(
            lax.slice_in_dim(block, block.shape[dim] - width, None, axis=dim), axis, forward
        )
        high = lax.ppermute(lax.slice_in_dim(block, 0, width, axis=dim), axis, backward)
        block = jnp.concatenate([low, block, high], axis=dim)
    return block


def near_block(padded, offsets, counts, points):
    rows = padded.shape[0]
    leaves = offsets.shape[0]
    blocks = padded.reshape(rows, -1, LEAF)
    index = offsets + HALO_LEAVES + jnp.arange(leaves, dtype=jnp.int32)[:, None]
    source = jnp.take(blocks, index.reshape(-1), axis=1).reshape(rows, leaves, NNEAR * LEAF)
    live = (jnp.arange(NNEAR, dtype=jnp.int32)[None, :] < counts[:, None]).astype(jnp.float32)
    live = jnp.repeat(live, LEAF, axis=1)
    target = points.reshape(3, leaves, LEAF)
    dist = jnp.zeros((leaves, LEAF, NNEAR * LEAF), jnp.float32)
    for comp in range(3):
        delta = target[comp][:, :, None] - source[comp][:, None, :]
        dist = dist + delta * delta
    tile = (source[3] * live)[:, None, :] * lax.rsqrt(dist + softening)
    return jnp.einsum("iab,rib->ria", tile, source[4:], precision=highest)


def per_device(
    densities,
    panels,
    areas,
    near_offsets,
    near_count,
    leaf_basis,
    local_trans,
    local_coupling,
    up_trans,
    coupling,
):
    width = HALO_LEAVES * LEAF
    stacked = jnp.concatenate([panels, areas[None, :], densities], 0)
    padded = with_halo(stacked, (("leaf", 1),), width)
    near = near_block(padded, near_offsets, near_count, panels)
    leaves = leaf_basis.shape[0]
    depth = leaves.bit_length() - 1
    leafx = densities.reshape(RHS, leaves, LEAF)
    moments = jnp.einsum("ilk,ril->ikr", leaf_basis, leafx, precision=highest)
    nearfar = []
    for level in range(depth):
        count = leaves >> level
        start = 2 * leaves - 2 * count
        transfer = local_trans[start : start + count]
        couple_local = local_coupling[start : start + count]
        sibling = moments.reshape(count // 2, 2, RANK, RHS)[:, ::-1].reshape(moments.shape)
        nearfar.append(jnp.einsum("nab,nbr->nar", couple_local, sibling, precision=highest))
        lifted = jnp.einsum("nba,nbr->nar", transfer, moments, precision=highest)
        moments = lifted.reshape(count // 2, 2, RANK, RHS).sum(1)
    coef = moments[0]
    trans = up_trans[0]
    couple = coupling[0]
    levels = up_trans.shape[1]
    farlist = []
    lifts = [coef]
    for level in range(levels - 1):
        lifts.append(jnp.dot(trans[level].T, lifts[-1], precision=highest))
    everyone = lax.all_gather(jnp.stack(lifts)[None], "leaf", axis=0, tiled=True)
    total = lax.axis_size("leaf")
    myself = lax.axis_index("leaf")
    for level in range(levels):
        grouped = everyone[:, level].reshape(total // 2**level, 2**level, RANK, RHS).sum(1)
        sibling = lax.dynamic_index_in_dim(
            grouped, jnp.bitwise_xor(myself // 2**level, 1), 0, keepdims=False
        )
        farlist.append(jnp.dot(couple[level], sibling, precision=highest))
    local = farlist[levels - 1]
    for level in range(levels - 1, 0, -1):
        local = farlist[level - 1] + jnp.dot(trans[level - 1], local, precision=highest)
    downward = local[None]
    for level in range(depth - 1, -1, -1):
        count = leaves >> level
        start = 2 * leaves - 2 * count
        transfer = local_trans[start : start + count]
        downward = nearfar[level] + jnp.einsum(
            "nab,nbr->nar", transfer, jnp.repeat(downward, 2, axis=0), precision=highest
        )
    far = jnp.einsum("ilk,ikr->ril", leaf_basis, downward, precision=highest)
    return (near + far).reshape(RHS, leaves * LEAF)


def solution(mesh):
    return jax.shard_map(
        per_device,
        mesh=mesh,
        in_specs=(
            P(None, "leaf"),
            P(None, "leaf"),
            P("leaf"),
            P("leaf", None),
            P("leaf"),
            P("leaf", None, None),
            P("leaf", None, None),
            P("leaf", None, None),
            P("leaf", None, None, None),
            P("leaf", None, None, None),
        ),
        out_specs=P(None, "leaf"),
        check_vma=False,
    )
```

profile of v0, /device:TPU:1, one launch (start us, length us, event | category | flops | bytes accessed | tf_op | source)
XLA Modules:
  0.0 177.4 jit_solution(16925365047421700621)
XLA Ops:
  8.9 2.4 %bitcast_reduce_fusion.7 = f32[16,64,16]{1,2,0:T(8,128)S(1)} fusion(f32[32,64,16]{1,2,0:T(8,128)S(1)} %fusion.38, f32[62,64,64]{2,1,0:T(8,128)} %param.16), kind=kOutput, calls=%fused_computation.61 | convolution fusion | flops 25182208 | bytes 1245184 | tf_op jit(solution)/shard_map/nba,nbr->nar/dot_general | solution.py:75
  12.0 1.6 bitcast_reduce_fusion.8
  16.6 1.7 constant_dynamic-update-slice_fusion.6
  23.5 1.4 pad_maximum_fusion.3
  24.8 4.6 %collective-permute-start = (f32[20,256]{1,0:T(8,128)}, f32[20,256]{1,0:T(8,128)}, u32[]{:S(2)}, u32[]{:S(2)}) collective-permute-start(f32[20,256]{1,0:T(8,128)} %get-tuple-element.20), channel_id=1, source_target_pairs={{0,1},{1,2},{2,3},{3,4},{4,5},{5,6},{6,7},{7,8},{8,9},{9,10},{10,1... | collective-permute-start | bytes 61448 | tf_op jit(solution)/shard_map/ppermute | solution.py:22
  29.4 2.4 %collective-permute-start.1 = (f32[20,256]{1,0:T(8,128)}, f32[20,256]{1,0:T(8,128)}, u32[]{:S(2)}, u32[]{:S(2)}) collective-permute-start(f32[20,256]{1,0:T(8,128)} %get-tuple-element.21), channel_id=1, source_target_pairs={{1,0},{2,1},{3,2},{4,3},{5,4},{6,5},{7,6},{8,7},{9,8},{10,9},{11,1... | collective-permute-start | bytes 61448 | tf_op jit(solution)/shard_map/ppermute | solution.py:25
  35.8 1.4 rev.16
  37.7 1.6 rev.14
  40.0 1.5 slice_reduce_fusion.6
  44.1 1.5 fusion.50
  45.7 1.7 fusion.45
  47.4 1.4 fusion.40
  48.7 2.5 %fusion.33 = f32[16,16,64]{2,1,0:T(8,128)} fusion(f32[16,64,16]{1,2,0:T(8,128)} %bitcast.245, f32[62,64,64]{2,1,0:T(8,128)S(1)} %copy-done.2), kind=kOutput, calls=%fused_computation.56 | convolution fusion | flops 12582912 | bytes 655360 | tf_op jit(solution)/shard_map/nab,nbr->nar/dot_general | solution.py:74
  51.2 2.7 %fusion.27 = f32[32,16,64]{2,1,0:T(8,128)S(1)} fusion(f32[32,64,16]{1,2,0:T(8,128)} %bitcast.242, f32[62,64,64]{2,1,0:T(8,128)S(1)} %copy-done.2), kind=kOutput, calls=%fused_computation.50 | convolution fusion | flops 25165824 | bytes 1310720 | tf_op jit(solution)/shard_map/nab,nbr->nar/dot_general | solution.py:74
  55.7 1.4 sub.84
  58.1 2.3 %gather_fusion = f32[192,20,64]{2,1,0:T(8,128)} fusion(f32[20,40,64]{2,0,1:T(8,128)S(1)} %copy.29, s32[1024]{0:T(1024)S(1)} %pad_clamp_fusion), kind=kCustom, calls=%fused_computation | custom fusion | bytes 1966848 | tf_op jit(solution)/shard_map/jit(_take)/gather | solution.py:35
  60.5 1.9 %select_bitcast_fusion = f32[20,192,64]{2,0,1:T(8,128)S(1)} fusion(f32[192,20,64]{2,1,0:T(8,128)} %gather_fusion, pred[192]{0:T(512)(128)(4,1)S(1)} %copy-done.13), kind=kLoop, calls=%fused_computation.13 | loop fusion | flops 245760 | bytes 1966272 | tf_op jit(solution)/shard_map/jit(_take)/select_n | solution.py:35
  64.1 1.6 copy.30
  65.7 1.8 %slice.169 = f32[16,32,384]{2,1,0:T(8,128)S(1)} reshape(f32[16,192,64]{2,1,0:T(8,128)} %copy.30) | data formatting | bytes 1572864 | tf_op jit(solution)/shard_map/slice | solution.py:44
  67.6 4.8 %fusion = f32[32,16,64]{2,1,0:T(8,128)S(1)} fusion(f32[32,384]{1,0:T(8,128)S(1)} %sub.86, f32[32,64]{1,0:T(8,128)S(1)} %copy-done.12, f32[32,384]{1,0:T(8,128)S(1)} %sub.81, f32[32,64]{1,0:T(8,128)S(1)} %sub.79, f32[32,384]{1,0:T(8,128)S(1)} %sub.76, f32[32,64]{1,0:T(8,128)S(1)} %sub.74, f32[32,384]{1,0:T(8,128)S(1)} %mul.24, f32[16,32,384]{2,1,0:T(8,128)S(1)} %slice.169), kind=kOutput, calls=%fused_computation.1 | convolution fusion | flops 158859264 | bytes 1138688 | tf_op jit(solution)/shard_map/iab,rib->ria/dot_general | solution.py:44
  72.4 80.3 %all-gather.3.cloned.1.call-done = f32[2048,64,16]{1,2,0:T(8,128)} async-done(((f32[8,64,16]{1,2,0:T(8,128)}), f32[2048,64,16]{1,2,0:T(8,128)}) %all-gather.3.cloned.1.call-update) | async-done | bytes 8388624 | tf_op jit(solution)/shard_map/all_gather | solution.py:85
  152.7 6.7 %fusion.141 = (f32[256,1,64,16]{2,3,1,0:T(8,128)S(1)}, f32[256,1,64,16]{2,3,1,0:T(8,128)S(1)}, f32[256,1,64,16]{2,3,1,0:T(8,128)S(1)}, f32[256,1,64,16]{2,3,1,0:...) fusion(f32[256,8,64,16]{2,3,1,0:T(8,128)} %bitcast.231), kind=kLoop, calls=%fused_computation.192 | loop fusion | bytes 16777216 | tf_op jit(solution)/shard_map/slice | solution.py:89
  166.2 1.7 convolution_add_fusion.1
  167.9 1.7 fusion.20
  (100 shorter events, 30.9 us)
Async XLA Ops:
  6.5 1.3 copy-start
  6.5 146.2 %all-gather.3.cloned.1.call-start = ((), (), s32[]{:S(2)}) async-start(), calls=%async_computation | async-start | bytes 16842752 | tf_op jit(solution)/shard_map/all_gather | solution.py:85
  7.8 10.4 %copy-start.5 = (f32[1,8,64,64]{3,2,1,0:T(8,128)S(1)}, f32[1,8,64,64]{3,2,1,0:T(8,128)}, u32[]{:S(2)}) copy-start(f32[1,8,64,64]{3,2,1,0:T(8,128)} %param.18) | copy-start | bytes 393220
  7.8 15.6 %copy-start.3 = (f32[16,2048]{1,0:T(8,128)S(1)}, f32[16,2048]{1,0:T(8,128)}, u32[]{:S(2)}) copy-start(f32[16,2048]{1,0:T(8,128)} %param.10) | copy-start | bytes 393220
  8.9 35.2 %copy-start.2 = (f32[62,64,64]{2,1,0:T(8,128)S(1)}, f32[62,64,64]{2,1,0:T(8,128)}, u32[]{:S(2)}) copy-start(f32[62,64,64]{2,1,0:T(8,128)} %param.17) | copy-start | bytes 3047428
  11.3 0.7 copy-start.4
  14.9 0.6 copy-start.8
  24.8 32.3 %collective-permute-start = (f32[20,256]{1,0:T(8,128)}, f32[20,256]{1,0:T(8,128)}, u32[]{:S(2)}, u32[]{:S(2)}) collective-permute-start(f32[20,256]{1,0:T(8,128)} %get-tuple-element.20), channel_id=1, source_target_pairs={{0,1},{1,2},{2,3},{3,4},{4,5},{5,6},{6,7},{7,8},{8,9},{9,10},{10,1... | collective-permute-start | bytes 61448 | tf_op jit(solution)/shard_map/ppermute | solution.py:22
  29.4 27.7 %collective-permute-start.1 = (f32[20,256]{1,0:T(8,128)}, f32[20,256]{1,0:T(8,128)}, u32[]{:S(2)}, u32[]{:S(2)}) collective-permute-start(f32[20,256]{1,0:T(8,128)} %get-tuple-element.21), channel_id=1, source_target_pairs={{1,0},{2,1},{3,2},{4,3},{5,4},{6,5},{7,6},{8,7},{9,8},{10,9},{11,1... | collective-permute-start | bytes 61448 | tf_op jit(solution)/shard_map/ppermute | solution.py:25
  58.1 2.3 %copy-start.13 = (pred[192]{0:T(512)(128)(4,1)S(1)}, pred[192]{0:T(512)(128)(4,1)}, u32[]{:S(2)}) copy-start(pred[192]{0:T(512)(128)(4,1)} %compare_and_fusion) | copy-start | bytes 580
  64.1 3.5 %copy-start.12 = (f32[32,64]{1,0:T(8,128)S(1)}, f32[32,64]{1,0:T(8,128)}, u32[]{:S(2)}) copy-start(f32[32,64]{1,0:T(8,128)} %sub.84) | copy-start | bytes 24580
  160.5 1.0 copy-start.9
  160.5 1.3 copy-start.6
  160.5 3.5 %copy-start.1 = (f32[62,64,64]{2,1,0:T(8,128)S(1)}, f32[62,64,64]{2,1,0:T(8,128)}, u32[]{:S(2)}) copy-start(f32[62,64,64]{2,1,0:T(8,128)} %param.16) | copy-start | bytes 3047428
  160.5 3.5 %copy-start.11 = (f32[2,16,64]{2,1,0:T(8,128)S(1)}, f32[2,16,64]{2,1,0:T(8,128)}, u32[]{:S(2)}) copy-start(f32[2,16,64]{2,1,0:T(8,128)} %fusion.50) | copy-start | bytes 24580
  160.5 3.8 %copy-start.10 = (f32[4,16,64]{2,1,0:T(8,128)S(1)}, f32[4,16,64]{2,1,0:T(8,128)}, u32[]{:S(2)}) copy-start(f32[4,16,64]{2,1,0:T(8,128)} %fusion.45) | copy-start | bytes 49156
  160.6 4.6 %copy-start.7 = (f32[16,16,64]{2,1,0:T(8,128)S(1)}, f32[16,16,64]{2,1,0:T(8,128)}, u32[]{:S(2)}) copy-start(f32[16,16,64]{2,1,0:T(8,128)} %fusion.33) | copy-start | bytes 196612
Sparse Core Ops, SparseCore 0:
  23.6 129.1 all-gather.2
where the time goes:
time: 178 us; the launch traced here: 177 us
  waiting for transfers between devices  80.3 us (45%)
  matrix products  36.8 us (21%)
  local copies, waits for them, and re-layouts  30.1 us (17%)
  between operations  13.9 us (8%)
  other arithmetic  9.3 us (5%)
  starting transfers between devices  7.01 us (4%)
    all_gather x1, waiting for transfers between devices, per_device(): lax.all_gather(jnp.stack(lifts)[None], 'leaf', axis=0, tiled=True)  80.3 us
    dot_general x5, matrix products, per_device(): jnp.einsum('nab,nbr->nar', couple_local, sibling, precision=highest)  9.75 us
    dot_general x5, matrix products, per_device(): lifted = jnp.einsum('nba,nbr->nar', transfer, moments, precision=highest)  8.04 us
    slice x1, local copies, waits for them, and re-layouts, per_device(): everyone[:, level].reshape(total // 2 ** level, 2 ** level, RANK, RHS)  6.7 us
    dot_general x7, matrix products, per_device(): lifts.append(jnp.dot(trans[level].T, lifts[-1], precision=highest))  5.16 us
    dot_general x1, matrix products, near_block(): return jnp.einsum('iab,rib->ria', tile, source[4:], precision=highest)  4.78 us
    ppermute x1, starting transfers between devices, with_halo(): lax.ppermute(lax.slice_in_dim(block, block.shape[dim] - width, None, axis...  4.58 us
    rev x4, local copies, waits for them, and re-layouts, per_device(): moments.reshape(count // 2, 2, RANK, RHS)[:, ::-1].reshape(moments.shape)  4.26 us
  transfers between devices with their start and end apart: 3, of which 1 were waited for; matrix products, arithmetic and copies ran while one was open for 24% of the time, Pallas kernels for 0%

commit v1 on v0

v1 whole, which is shorter than its diff:
```python
import jax
import jax.numpy as jnp
from jax import lax
from jax.experimental import pallas as pl
from jax.experimental.pallas import tpu as pltpu
from jax.sharding import PartitionSpec as P

LEAF = 64
RANK = 64
RHS = 16
LEAVES = 32
HALO = 4
NNEAR = 6
LEVELS = 8
DEPTH = 5
NODES = 256
SPAN = LEAVES * LEAF
softening = 0.25
MESH = pl.DeviceIdType.MESH
f32 = jnp.float32
bf16 = jnp.bfloat16

PHASES = ((0, 3), (3, 2), (5, 3))
START = [2 * LEAVES - 2 * (LEAVES >> j) for j in range(DEPTH)]
PAIR = [s // 2 for s in START]


def split(x):
    high = x.astype(bf16)
    return high, (x - high.astype(f32)).astype(bf16)


def dot(a, b):
    return lax.dot_general(a, b, (((1,), (0,)), ((), ())), preferred_element_type=f32)


def dot_t(a, b):
    return lax.dot_general(a, b, (((1,), (1,)), ((), ())), preferred_element_type=f32)


def product(a, b, op):
    ah, al = a
    bh, bl = b
    rows = ah.shape[0]
    both = op(jnp.concatenate([ah, al], 0), bh)
    return both[:rows] + (both[rows:] + op(ah, bl))


def sweep(count, body, unroll):
    if count <= unroll:
        for i in range(count):
            body(i)
        return

    def step(i, carry):
        for u in range(unroll):
            body(i * unroll + u)
        return carry

    lax.fori_loop(0, count // unroll, step, 0)


def rows_at(index, count):
    if isinstance(index, int):
        return slice(index * count, (index + 1) * count)
    return pl.ds(pl.multiple_of(index * count, count), count)


def kernel(
    dens_hbm, pan_hbm, area_hbm, off_ref, cnt_ref, bas_hbm, ltr_hbm, lco_hbm, upt_hbm, cpl_hbm,
    out_ref,
    dens, pan, area, bas, ltr, lco, upt, cpl,
    bas_h, bas_l, ltr_h, ltr_l, gch, gcl, dh, dl,
    blocks, points, qrow, gpair, hpair, acc,
    wt1h, wt1l, wt2h, wt2l, wt3h, wt3l, wk_h, wk_l,
    send, recv, load_sem, send_sem, recv_sem, halo_ssem, halo_rsem,
):
    me = lax.axis_index("leaf")
    right = lax.rem(me + 1, NODES)
    left = lax.rem(me + NODES - 1, NODES)
    barrier = pltpu.get_barrier_semaphore()
    peers = [p << first for first, levels in PHASES for p in range(1, 1 << levels)]
    for p in peers:
        pl.semaphore_signal(barrier, inc=1, device_id=(me ^ p,), device_id_type=MESH)
    for neighbour in (left, right):
        pl.semaphore_signal(barrier, inc=1, device_id=(neighbour,), device_id_type=MESH)

    loads = {}
    for at, (name, src, dst) in enumerate(
        (
            ("dens", dens_hbm, dens),
            ("bas", bas_hbm, bas),
            ("ltr", ltr_hbm, ltr),
            ("upt", upt_hbm, upt),
            ("pan", pan_hbm, pan),
            ("area", area_hbm, area),
            ("lco", lco_hbm, lco),
            ("cpl", cpl_hbm, cpl),
        )
    ):
        loads[name] = pltpu.make_async_copy(src, dst, load_sem.at[at])
        loads[name].start()

    lane = lax.broadcasted_iota(jnp.int32, (1, 2 * LEAF), 1)
    low = lane < LEAF
    half = jnp.zeros((RHS, LEAF), f32)

    loads["dens"].wait()
    loads["bas"].wait()

    def moments(p):
        x = dens[:, rows_at(p, 2 * LEAF)]
        x = jnp.concatenate([jnp.where(low, x, 0.0), jnp.where(low, 0.0, x)], 0)
        w = split(bas[rows_at(p, 2)].reshape(2 * LEAF, RANK))
        bas_h[rows_at(p, 2 * LEAF)] = w[0]
        bas_l[rows_at(p, 2 * LEAF)] = w[1]
        qrow[p] = product(split(x), w, dot)

    sweep(LEAVES // 2, moments, 4)
    loads["ltr"].wait()

    def lift(level, p):
        q = qrow[PAIR[level] + p]
        q = jnp.concatenate([q[:RHS], q[RHS:]], 1)
        at = PAIR[level] + p
        w = split(ltr[rows_at(at, 2)].reshape(2 * RANK, RANK))
        ltr_h[rows_at(at, 2 * RANK)] = w[0]
        ltr_l[rows_at(at, 2 * RANK)] = w[1]
        return product(split(q), w, dot)

    for level in range(DEPTH - 1):

        def lift_two(m, level=level):
            qrow[PAIR[level + 1] + m] = jnp.concatenate(
                [lift(level, 2 * m), lift(level, 2 * m + 1)], 0
            )

        sweep(LEAVES >> (level + 2), lift_two, 4)
    loads["upt"].wait()

    e = [split(upt[0, k]) for k in range(LEVELS - 1)]
    zero = jnp.zeros((RANK, RANK), f32)

    def chain(first, count):
        out = [upt[0, first]]
        for k in range(first + 1, first + count):
            out.append(product(split(out[-1]), e[k], dot))
        return out

    t1, t2, t3 = chain(0, 3)
    wt1h[...], wt1l[...] = split(jnp.concatenate([t3, zero, t3, t1, t3, t2], 1))
    coef = lift(DEPTH - 1, 0)

    def exchange(phase, messages):
        first, levels = PHASES[phase]
        base = sum((1 << n) - 1 for _, n in PHASES[:phase])
        slot = sum(n for _, n in PHASES[:phase])
        for k in range(levels):
            send[slot + k] = messages[k]
        copies = []
        for p in reversed(range(1, 1 << levels)):
            copy = pltpu.make_async_remote_copy(
                src_ref=send.at[slot + p.bit_length() - 1],
                dst_ref=recv.at[base + p - 1],
                send_sem=send_sem.at[base + p - 1],
                recv_sem=recv_sem.at[base + p - 1],
                device_id=(me ^ (p << first),),
                device_id_type=MESH,
            )
            copy.start()
            copies.append(copy)

        def receive():
            for copy in copies:
                copy.wait()
            sums = []
            for k in range(levels):
                parts = [recv[base + p - 1] for p in range(1 << k, 2 << k)]
                while len(parts) > 1:
                    parts = [a + b for a, b in zip(parts[::2], parts[1::2])]
                sums.append(parts[0])
            return sums

        return receive

    own = product(split(coef), (wt1h[...], wt1l[...]), dot)
    own = [own[:, 2 * RANK * k : 2 * RANK * (k + 1)] for k in range(3)]
    own[0] = own[0] + jnp.concatenate([half, coef], 1)
    pl.semaphore_wait(barrier, len(peers) + 2)
    receive = exchange(0, own)

    loads["pan"].wait()
    loads["area"].wait()
    halo_rows = jnp.zeros((5, 2 * LEAF), f32)

    def pack(p):
        at = rows_at(p, 2 * LEAF)
        coords = jnp.concatenate([pan[:, at], halo_rows], 0)
        tile = jnp.concatenate([dens[:, at] * area[:, at], coords], 0)
        blocks[HALO + 2 * p] = tile
        blocks[HALO + 2 * p + 1] = pltpu.roll(tile, LEAF, 1)
        points[at, :] = coords.T

    sweep(LEAVES // 2, pack, 4)
    halos = []
    for at, (source, target, device) in enumerate(
        ((LEAVES, 0, right), (HALO, HALO + LEAVES, left))
    ):
        copy = pltpu.make_async_remote_copy(
            src_ref=blocks.at[pl.ds(source, HALO)],
            dst_ref=blocks.at[pl.ds(target, HALO)],
            send_sem=halo_ssem.at[at],
            recv_sem=halo_rsem.at[at],
            device_id=(device,),
            device_id_type=MESH,
        )
        copy.start()
        halos.append(copy)

    u4, u5 = chain(3, 2)
    wt2h[...], wt2l[...] = split(jnp.concatenate([u5, zero, u5, u4], 1))
    v6, v7 = chain(5, 2)
    wt3h[...], wt3l[...] = split(jnp.concatenate([zero, v6, v7, zero], 1))
    loads["cpl"].wait()
    t4 = product(split(t3), e[3], dot)
    t5 = product(split(t3), split(u5), dot)
    t6 = product(split(t5), e[5], dot)
    t7 = product(split(t5), split(v7), dot)
    blank = jnp.zeros((RANK, RANK), bf16)
    wk_h[:, rows_at(LEVELS, RANK)] = blank
    wk_l[:, rows_at(LEVELS, RANK)] = blank
    for k, t in enumerate((None, t1, t2, t3, t4, t5, t6, t7)):
        w = cpl[0, k] if t is None else product(split(t), split(cpl[0, k]), dot)
        wk_h[:, rows_at(k, RANK)], wk_l[:, rows_at(k, RANK)] = split(w)

    loads["lco"].wait()

    def couple(p):
        q = qrow[p]
        q = jnp.concatenate([q[RHS:], q[:RHS]], 0)
        w = split(lco[rows_at(p, 2)].reshape(2 * RANK, RANK))
        g = product(split(q), w, dot_t)
        gpair[p] = jnp.where(low, g[:RHS], g[RHS:])

    sweep(28, couple, 4)
    for p in range(28, 31):
        couple(p)

    sums = receive()
    tot = own[0] + (sums[0] + (sums[1] + sums[2]))
    coef = tot[:, :RANK]
    early = [s[:, RANK:] for s in sums]
    own = product(split(coef), (wt2h[...], wt2l[...]), dot)
    own = [own[:, 2 * RANK * k : 2 * RANK * (k + 1)] for k in range(2)]
    own[0] = own[0] + jnp.concatenate([half, coef], 1)
    receive = exchange(1, own)

    hpair[PAIR[4]] = gpair[PAIR[4]]

    for level in range(DEPTH - 2, -1, -1):

        def lower_two(m, level=level):
            parent = hpair[PAIR[level + 1] + m]
            for c in range(2):
                at = PAIR[level] + 2 * m + c
                w = (ltr_h[rows_at(at, 2 * RANK)], ltr_l[rows_at(at, 2 * RANK)])
                h = split(parent[:, RANK * c : RANK * (c + 1)])
                hpair[at] = gpair[at] + product(h, w, dot_t)

        sweep(LEAVES >> (level + 2), lower_two, 4)

    def far_leaf(p):
        h = hpair[p]
        h = jnp.concatenate([h[:, :RANK], h[:, RANK:]], 0)
        w = (bas_h[rows_at(p, 2 * LEAF)], bas_l[rows_at(p, 2 * LEAF)])
        far = product(split(h), w, dot_t)
        acc[:, rows_at(p, 2 * LEAF)] = jnp.where(low, far[:RHS], far[RHS:])

    sweep(LEAVES // 2, far_leaf, 4)

    for copy in halos:
        copy.wait()
    for target, edge in ((0, 0), (HALO + LEAVES, NODES - 1)):
        keep = jnp.where(me == edge, 0.0, 1.0)
        for j in range(target, target + HALO):
            blocks[j] = blocks[j] * keep

    def near_leaf(i):
        at = rows_at(i, LEAF)
        tx, ty, tz = (points[at, c : c + 1] for c in range(3))
        count = cnt_ref[i]
        kernels, charges = [], []
        for t in range(NNEAR // 2):
            j0 = off_ref[i, 2 * t] + (i + HALO)
            j1 = off_ref[i, 2 * t + 1] + (i + HALO)
            c = jnp.where(low, blocks[j0], blocks[j1 ^ 1])
            live = jnp.where(low, 2 * t, 2 * t + 1) < count
            charges.append(jnp.where(live, c[:RHS], 0.0))
            dx = tx - c[RHS : RHS + 1]
            dy = ty - c[RHS + 1 : RHS + 2]
            dz = tz - c[RHS + 2 : RHS + 3]
            kernels.append(lax.rsqrt(dx * dx + dy * dy + dz * dz + softening))
        return product(
            split(jnp.concatenate(charges, 1)), split(jnp.concatenate(kernels, 1)), dot_t
        )

    def near(p):
        tile = jnp.concatenate([near_leaf(2 * p), near_leaf(2 * p + 1)], 1)
        at = rows_at(p, 2 * LEAF)
        acc[:, at] = acc[:, at] + tile

    def near_some(first, last):
        lax.fori_loop(first, last, lambda p, carry: (near(p), carry)[1], 0)

    near_some(0, 4)

    sums = receive()
    tot = own[0] + (sums[0] + sums[1])
    coef = tot[:, :RANK]
    early += [s[:, RANK:] for s in sums]
    own = product(split(coef), (wt3h[...], wt3l[...]), dot)
    own = [jnp.concatenate([coef, half], 1), own[:, : 2 * RANK], own[:, 2 * RANK :]]
    receive = exchange(2, own)

    local = half
    for k in range(5):
        w = (wk_h[:, rows_at(k, RANK)], wk_l[:, rows_at(k, RANK)])
        local = local + product(split(early[k]), w, dot_t)

    top = rows_at(PAIR[4], 2 * RANK)
    gch[top] = ltr_h[top]
    gcl[top] = ltr_l[top]
    for level in range(DEPTH - 2, -1, -1):

        def compose(m, level=level):
            at = rows_at(PAIR[level] + m, 2 * RANK)
            up = rows_at(START[level + 1] + m, RANK)
            gch[at], gcl[at] = split(
                product((ltr_h[at], ltr_l[at]), (gch[up], gcl[up]), dot)
            )

        sweep(LEAVES >> (level + 1), compose, 4)

    def compose_leaf(i):
        at = rows_at(i, LEAF)
        dh[at], dl[at] = split(product((bas_h[at], bas_l[at]), (gch[at], gcl[at]), dot))

    sweep(LEAVES, compose_leaf, 4)
    near_some(4, 16)

    s5, s6, s7 = receive()
    tail = split(jnp.concatenate([s5 + s6, s7], 1))
    w = (wk_h[:, 5 * RANK :], wk_l[:, 5 * RANK :])
    local = split(local + product(tail, w, dot_t))
    for b in range(SPAN // 256):
        at = rows_at(b, 256)
        out_ref[:, at] = acc[:, at] + product(local, (dh[at], dl[at]), dot_t)


def per_device(
    densities, panels, areas, near_offsets, near_count,
    leaf_basis, local_trans, local_coupling, up_trans, coupling,
):
    hbm = pl.BlockSpec(memory_space=pltpu.HBM)
    smem = pl.BlockSpec(memory_space=pltpu.SMEM)
    nlocal = 2 * LEAVES - 2
    npeers = sum((1 << n) - 1 for _, n in PHASES)
    vm = pltpu.VMEM
    scratch = [
        vm((RHS, SPAN), f32),
        vm((3, SPAN), f32),
        vm((1, SPAN), f32),
        vm((LEAVES, LEAF, RANK), f32),
        vm((nlocal, RANK, RANK), f32),
        vm((nlocal, RANK, RANK), f32),
        vm((1, LEVELS, RANK, RANK), f32),
        vm((1, LEVELS, RANK, RANK), f32),
        vm((SPAN, RANK), bf16),
        vm((SPAN, RANK), bf16),
        vm((nlocal * RANK, RANK), bf16),
        vm((nlocal * RANK, RANK), bf16),
        vm((nlocal * RANK, RANK), bf16),
        vm((nlocal * RANK, RANK), bf16),
        vm((SPAN, RANK), bf16),
        vm((SPAN, RANK), bf16),
        vm((LEAVES + 2 * HALO, 24, 2 * LEAF), f32),
        vm((SPAN, 8), f32),
        vm((nlocal // 2, 2 * RHS, RANK), f32),
        vm((nlocal // 2, RHS, 2 * RANK), f32),
        vm((nlocal // 2, RHS, 2 * RANK), f32),
        vm((RHS, SPAN), f32),
        vm((RANK, 6 * RANK), bf16),
        vm((RANK, 6 * RANK), bf16),
        vm((RANK, 4 * RANK), bf16),
        vm((RANK, 4 * RANK), bf16),
        vm((RANK, 4 * RANK), bf16),
        vm((RANK, 4 * RANK), bf16),
        vm((RANK, 9 * RANK), bf16),
        vm((RANK, 9 * RANK), bf16),
        vm((LEVELS, RHS, 2 * RANK), f32),
        vm((npeers, RHS, 2 * RANK), f32),
        pltpu.SemaphoreType.DMA((8,)),
        pltpu.SemaphoreType.DMA((npeers,)),
        pltpu.SemaphoreType.DMA((npeers,)),
        pltpu.SemaphoreType.DMA((2,)),
        pltpu.SemaphoreType.DMA((2,)),
    ]
    return pl.pallas_call(
        kernel,
        out_shape=jax.ShapeDtypeStruct((RHS, SPAN), f32),
        in_specs=[hbm, hbm, hbm, smem, smem, hbm, hbm, hbm, hbm, hbm],
        out_specs=pl.BlockSpec(memory_space=pltpu.VMEM),
        scratch_shapes=scratch,
        compiler_params=pltpu.CompilerParams(
            collective_id=0, has_side_effects=True, vmem_limit_bytes=40 * 1024 * 1024
        ),
    )(
        densities, panels, areas.reshape(1, SPAN), near_offsets, near_count,
        leaf_basis, local_trans, local_coupling, up_trans, coupling,
    )


def solution(mesh):
    return jax.shard_map(
        per_device,
        mesh=mesh,
        in_specs=(
            P(None, "leaf"),
            P(None, "leaf"),
            P("leaf"),
            P("leaf", None),
            P("leaf"),
            P("leaf", None, None),
            P("leaf", None, None),
            P("leaf", None, None),
            P("leaf", None, None, None),
            P("leaf", None, None, None),
        ),
        out_specs=P(None, "leaf"),
        check_vma=False,
    )
```

time: 178 us -> 42 us (0.24)
  waiting for transfers between devices: 80.3 us -> 0 us
  matrix products: 36.8 us -> 0 us
  Pallas kernels: 0 us -> 30.9 us
  local copies, waits for them, and re-layouts: 30.1 us -> 10.7 us
  between operations: 13.9 us -> 0.02 us
  other arithmetic: 9.3 us -> 0 us
  starting transfers between devices: 7.01 us -> 0 us
    all_gather x1 -> x0, waiting for transfers between devices: 80.3 us -> none  [per_device(): lax.all_gather(jnp.stack(lifts)[None], 'leaf', axis=0, tiled=True)]
    dot_general x40 -> x0, matrix products: 36.8 us -> none  [the longest x5 9.75 us: per_device(): jnp.einsum('nab,nbr->nar', couple_local, sibling, precision=highest)]
    pallas_call x0 -> x1, Pallas kernels: none -> 30.9 us  [per_device(): pl.pallas_call(kernel, out_shape=jax.ShapeDtypeStruct((RHS, SPAN), f32),...]
    slice x6 -> x0, local copies, waits for them, and re-layouts: 13 us -> none  [the longest x1 6.7 us: per_device(): everyone[:, level].reshape(total // 2 ** level, 2 ** level, RANK, RHS)]
    unnamed x28 -> x20, local copies, waits for them, and re-layouts: 2.11 us -> 10.7 us
    ppermute x2 -> x0, starting transfers between devices: 7.01 us -> none  [the longest x1 4.58 us: with_halo(): lax.ppermute(lax.slice_in_dim(block, block.shape[dim] - width, None, axis...]
    rev x4 -> x0, local copies, waits for them, and re-layouts: 4.26 us -> none  [per_device(): moments.reshape(count // 2, 2, RANK, RHS)[:, ::-1].reshape(moments.shape)]
    reshape x8 -> x0, local copies, waits for them, and re-layouts: 4.04 us -> none  [the longest x2 1.29 us: near_block(): index.reshape(-1)]
  transfers between devices with their start and end apart: 3 -> 0, of which waited for: 1 -> 0; matrix products, arithmetic and copies ran while one was open for 24% -> 0% of each run, Pallas kernels for 0% -> 0%
where the time goes in v1:
time: 42 us; the launch traced here: 41.6 us
  Pallas kernels  30.9 us (74%)
  local copies, waits for them, and re-layouts  10.7 us (25%)
    pallas_call x1, Pallas kernels, per_device(): pl.pallas_call(kernel, out_shape=jax.ShapeDtypeStruct((RHS, SPAN), f32),...  30.9 us
    unnamed x20, local copies, waits for them, and re-layouts  10.7 us

profile of v1, /device:TPU:1, one launch (start us, length us, event | category | flops | bytes accessed | tf_op | source)
XLA Modules:
  0.0 41.6 jit_solution(6381149966301868084)
XLA Ops:
  0.0 0.8 %copy.11.off_ref = s32[32,6]{1,0:T(8,128)S(1)} copy(s32[32,6]{0,1:T(8,128)} %param.13) | data formatting | bytes 1536 | tf_op args[3]
  0.8 0.0 copy-start
  0.8 1.6 %copy-done = f32[62,64,64]{2,1,0:T(8,128)S(1)} copy-done((f32[62,64,64]{2,1,0:T(8,128)S(1)}, f32[62,64,64]{2,1,0:T(8,128)}, u32[]{:S(2)}) %copy-start) | copy-done | bytes 1015832
  2.3 0.0 copy-start.1
  2.3 1.6 %copy-done.1 = f32[62,64,64]{2,1,0:T(8,128)S(1)} copy-done((f32[62,64,64]{2,1,0:T(8,128)S(1)}, f32[62,64,64]{2,1,0:T(8,128)}, u32[]{:S(2)}) %copy-start.1) | copy-done | bytes 1015832
  3.9 0.0 copy-start.2
  3.9 1.2 %copy-done.2 = f32[32,64,64]{2,1,0:T(8,128)S(1)} copy-done((f32[32,64,64]{2,1,0:T(8,128)S(1)}, f32[32,64,64]{2,1,0:T(8,128)}, u32[]{:S(2)}) %copy-start.2) | copy-done | bytes 524312
  5.1 0.0 copy-start.3
  5.1 0.9 %copy-done.3 = f32[1,8,64,64]{3,2,1,0:T(8,128)S(1)} copy-done((f32[1,8,64,64]{3,2,1,0:T(8,128)S(1)}, f32[1,8,64,64]{3,2,1,0:T(8,128)}, u32[]{:S(2)}) %copy-start.3) | copy-done | bytes 131096
  6.1 0.0 copy-start.4
  6.1 0.9 %copy-done.4 = f32[1,8,64,64]{3,2,1,0:T(8,128)S(1)} copy-done((f32[1,8,64,64]{3,2,1,0:T(8,128)S(1)}, f32[1,8,64,64]{3,2,1,0:T(8,128)}, u32[]{:S(2)}) %copy-start.4) | copy-done | bytes 131096
  7.0 0.0 copy-start.5
  7.0 0.9 %copy-done.5 = f32[16,2048]{1,0:T(8,128)S(1)} copy-done((f32[16,2048]{1,0:T(8,128)S(1)}, f32[16,2048]{1,0:T(8,128)}, u32[]{:S(2)}) %copy-start.5) | copy-done | bytes 131096
  7.9 0.0 copy-start.6
  7.9 0.8 %copy-done.6 = f32[3,2048]{1,0:T(4,128)S(1)} copy-done((f32[3,2048]{1,0:T(4,128)S(1)}, f32[3,2048]{1,0:T(4,128)}, u32[]{:S(2)}) %copy-start.6) | copy-done | bytes 24600
  8.7 0.0 copy-start.7
  8.7 0.7 %copy-done.7 = f32[2048]{0:T(1024)S(1)} copy-done((f32[2048]{0:T(1024)S(1)}, f32[2048]{0:T(1024)}, u32[]{:S(2)}) %copy-start.7) | copy-done | bytes 8216
  9.4 0.0 copy-start.8
  9.4 0.7 %copy-done.8 = s32[32]{0:T(128)S(1)} copy-done((s32[32]{0:T(128)S(1)}, s32[32]{0:T(128)}, u32[]{:S(2)}) %copy-start.8) | copy-done | bytes 152
  10.0 30.9 %shard_map.100 = f32[16,2048]{1,0:T(8,128)S(1)} custom-call(f32[16,2048]{1,0:T(8,128)S(1)} %copy-done.5, f32[3,2048]{1,0:T(4,128)S(1)} %copy-done.6, f32[1,2048]{1,0:T(1,128)S(1)} %bitcast.1, s32[32,6]{1,0:T(8,128)S(1)} %copy.11.off_ref, s32[32]{0:T(128)S(1)} %copy-done.8, f32[32,64,64]{2,1,0:T(8,128)S(1)} %copy-done.2, f32[62,64,64]{2,1,0:T(8,128)S(1)} %copy-done, ...), custom_call_target="tpu_custom_call" | custom-call | tf_op jit(solution)/shard_map/pallas_call | solution.py:408
  40.9 0.7 %copy.13 = f32[16,2048]{1,0:T(8,128)} copy(f32[16,2048]{1,0:T(8,128)S(1)} %shard_map.100) | data formatting | bytes 262144
Async XLA Ops:
  0.8 1.6 %copy-start = (f32[62,64,64]{2,1,0:T(8,128)S(1)}, f32[62,64,64]{2,1,0:T(8,128)}, u32[]{:S(2)}) copy-start(f32[62,64,64]{2,1,0:T(8,128)} %ltr_hbm.1) | copy-start | bytes 3047428
  2.3 1.6 %copy-start.1 = (f32[62,64,64]{2,1,0:T(8,128)S(1)}, f32[62,64,64]{2,1,0:T(8,128)}, u32[]{:S(2)}) copy-start(f32[62,64,64]{2,1,0:T(8,128)} %lco_hbm.1) | copy-start | bytes 3047428
  3.9 1.2 %copy-start.2 = (f32[32,64,64]{2,1,0:T(8,128)S(1)}, f32[32,64,64]{2,1,0:T(8,128)}, u32[]{:S(2)}) copy-start(f32[32,64,64]{2,1,0:T(8,128)} %bas_hbm.1) | copy-start | bytes 1572868
  5.1 0.9 %copy-start.3 = (f32[1,8,64,64]{3,2,1,0:T(8,128)S(1)}, f32[1,8,64,64]{3,2,1,0:T(8,128)}, u32[]{:S(2)}) copy-start(f32[1,8,64,64]{3,2,1,0:T(8,128)} %upt_hbm.1) | copy-start | bytes 393220
  6.1 0.9 %copy-start.4 = (f32[1,8,64,64]{3,2,1,0:T(8,128)S(1)}, f32[1,8,64,64]{3,2,1,0:T(8,128)}, u32[]{:S(2)}) copy-start(f32[1,8,64,64]{3,2,1,0:T(8,128)} %cpl_hbm.1) | copy-start | bytes 393220
  7.0 0.9 %copy-start.5 = (f32[16,2048]{1,0:T(8,128)S(1)}, f32[16,2048]{1,0:T(8,128)}, u32[]{:S(2)}) copy-start(f32[16,2048]{1,0:T(8,128)} %dens_hbm.1) | copy-start | bytes 393220
  7.9 0.8 %copy-start.6 = (f32[3,2048]{1,0:T(4,128)S(1)}, f32[3,2048]{1,0:T(4,128)}, u32[]{:S(2)}) copy-start(f32[3,2048]{1,0:T(4,128)} %pan_hbm.1) | copy-start | bytes 73732
  8.7 0.7 %copy-start.7 = (f32[2048]{0:T(1024)S(1)}, f32[2048]{0:T(1024)}, u32[]{:S(2)}) copy-start(f32[2048]{0:T(1024)} %param.12) | copy-start | bytes 24580
  9.4 0.7 %copy-start.8 = (s32[32]{0:T(128)S(1)}, s32[32]{0:T(128)}, u32[]{:S(2)}) copy-start(s32[32]{0:T(128)} %cnt_ref.1) | copy-start | bytes 388

commit v2 on v1

--- a/solution.py
+++ b/solution.py
@@ -67,24 +67,17 @@
 
 
 def kernel(
-    dens_hbm, pan_hbm, area_hbm, off_ref, cnt_ref, bas_hbm, ltr_hbm, lco_hbm, upt_hbm, cpl_hbm,
-    out_ref,
-    dens, pan, area, bas, ltr, lco, upt, cpl,
+    dens_hbm, pan_hbm, area_hbm, off_hbm, cnt_hbm, bas_hbm, ltr_hbm, lco_hbm, upt_hbm, cpl_hbm,
+    out_hbm,
+    out_ref, off_ref, cnt_ref, dens, pan, area, bas, ltr, lco, upt, cpl,
     bas_h, bas_l, ltr_h, ltr_l, gch, gcl, dh, dl,
     blocks, points, qrow, gpair, hpair, acc,
     wt1h, wt1l, wt2h, wt2l, wt3h, wt3l, wk_h, wk_l,
-    send, recv, load_sem, send_sem, recv_sem, halo_ssem, halo_rsem,
+    send, recv, load_sem, store_sem, send_sem, recv_sem, halo_ssem, halo_rsem,
 ):
     me = lax.axis_index("leaf")
     right = lax.rem(me + 1, NODES)
     left = lax.rem(me + NODES - 1, NODES)
-    barrier = pltpu.get_barrier_semaphore()
-    peers = [p << first for first, levels in PHASES for p in range(1, 1 << levels)]
-    for p in peers:
-        pl.semaphore_signal(barrier, inc=1, device_id=(me ^ p,), device_id_type=MESH)
-    for neighbour in (left, right):
-        pl.semaphore_signal(barrier, inc=1, device_id=(neighbour,), device_id_type=MESH)
-
     loads = {}
     for at, (name, src, dst) in enumerate(
         (
@@ -94,12 +87,21 @@
             ("upt", upt_hbm, upt),
             ("pan", pan_hbm, pan),
             ("area", area_hbm, area),
+            ("off", off_hbm, off_ref),
+            ("cnt", cnt_hbm, cnt_ref),
             ("lco", lco_hbm, lco),
             ("cpl", cpl_hbm, cpl),
         )
     ):
         loads[name] = pltpu.make_async_copy(src, dst, load_sem.at[at])
         loads[name].start()
+
+    barrier = pltpu.get_barrier_semaphore()
+    peers = [p << first for first, levels in PHASES for p in range(1, 1 << levels)]
+    for p in peers:
+        pl.semaphore_signal(barrier, inc=1, device_id=(me ^ p,), device_id_type=MESH)
+    for neighbour in (left, right):
+        pl.semaphore_signal(barrier, inc=1, device_id=(neighbour,), device_id_type=MESH)
 
     lane = lax.broadcasted_iota(jnp.int32, (1, 2 * LEAF), 1)
     low = lane < LEAF
@@ -116,7 +118,7 @@
         bas_l[rows_at(p, 2 * LEAF)] = w[1]
         qrow[p] = product(split(x), w, dot)
 
-    sweep(LEAVES // 2, moments, 4)
+    sweep(LEAVES // 2, moments, 16)
     loads["ltr"].wait()
 
     def lift(level, p):
@@ -135,7 +137,7 @@
                 [lift(level, 2 * m), lift(level, 2 * m + 1)], 0
             )
 
-        sweep(LEAVES >> (level + 2), lift_two, 4)
+        sweep(LEAVES >> (level + 2), lift_two, 16)
     loads["upt"].wait()
 
     e = [split(upt[0, k]) for k in range(LEVELS - 1)]
@@ -201,7 +203,7 @@
         blocks[HALO + 2 * p + 1] = pltpu.roll(tile, LEAF, 1)
         points[at, :] = coords.T
 
-    sweep(LEAVES // 2, pack, 4)
+    sweep(LEAVES // 2, pack, 16)
     halos = []
     for at, (source, target, device) in enumerate(
         ((LEAVES, 0, right), (HALO, HALO + LEAVES, left))
@@ -242,7 +244,7 @@
         g = product(split(q), w, dot_t)
         gpair[p] = jnp.where(low, g[:RHS], g[RHS:])
 
-    sweep(28, couple, 4)
+    sweep(28, couple, 14)
     for p in range(28, 31):
         couple(p)
 
@@ -267,7 +269,7 @@
                 h = split(parent[:, RANK * c : RANK * (c + 1)])
                 hpair[at] = gpair[at] + product(h, w, dot_t)
 
-        sweep(LEAVES >> (level + 2), lower_two, 4)
+        sweep(LEAVES >> (level + 2), lower_two, 16)
 
     def far_leaf(p):
         h = hpair[p]
@@ -276,8 +278,10 @@
         far = product(split(h), w, dot_t)
         acc[:, rows_at(p, 2 * LEAF)] = jnp.where(low, far[:RHS], far[RHS:])
 
-    sweep(LEAVES // 2, far_leaf, 4)
-
+    sweep(LEAVES // 2, far_leaf, 16)
+
+    loads["off"].wait()
+    loads["cnt"].wait()
     for copy in halos:
         copy.wait()
     for target, edge in ((0, 0), (HALO + LEAVES, NODES - 1)):
@@ -291,8 +295,8 @@
         count = cnt_ref[i]
         kernels, charges = [], []
         for t in range(NNEAR // 2):
-            j0 = off_ref[i, 2 * t] + (i + HALO)
-            j1 = off_ref[i, 2 * t + 1] + (i + HALO)
+            j0 = off_ref[2 * t, i] + (i + HALO)
+            j1 = off_ref[2 * t + 1, i] + (i + HALO)
             c = jnp.where(low, blocks[j0], blocks[j1 ^ 1])
             live = jnp.where(low, 2 * t, 2 * t + 1) < count
             charges.append(jnp.where(live, c[:RHS], 0.0))
@@ -310,9 +314,9 @@
         acc[:, at] = acc[:, at] + tile
 
     def near_some(first, last):
-        lax.fori_loop(first, last, lambda p, carry: (near(p), carry)[1], 0)
-
-    near_some(0, 4)
+        lax.fori_loop(first // 2, last // 2, lambda p, carry: (near(2 * p), near(2 * p + 1), carry)[2], 0)
+
+    near_some(0, 8)
 
     sums = receive()
     tot = own[0] + (sums[0] + sums[1])
@@ -339,22 +343,27 @@
                 product((ltr_h[at], ltr_l[at]), (gch[up], gcl[up]), dot)
             )
 
-        sweep(LEAVES >> (level + 1), compose, 4)
+        sweep(LEAVES >> (level + 1), compose, 16)
 
     def compose_leaf(i):
         at = rows_at(i, LEAF)
         dh[at], dl[at] = split(product((bas_h[at], bas_l[at]), (gch[at], gcl[at]), dot))
 
-    sweep(LEAVES, compose_leaf, 4)
-    near_some(4, 16)
+    sweep(LEAVES, compose_leaf, 16)
+    near_some(8, 16)
 
     s5, s6, s7 = receive()
     tail = split(jnp.concatenate([s5 + s6, s7], 1))
     w = (wk_h[:, 5 * RANK :], wk_l[:, 5 * RANK :])
     local = split(local + product(tail, w, dot_t))
-    for b in range(SPAN // 256):
-        at = rows_at(b, 256)
+    stores = []
+    for b in range(4):
+        at = rows_at(b, 512)
         out_ref[:, at] = acc[:, at] + product(local, (dh[at], dl[at]), dot_t)
+        stores.append(pltpu.make_async_copy(out_ref.at[:, at], out_hbm.at[:, at], store_sem.at[b]))
+        stores[-1].start()
+    for copy in stores:
+        copy.wait()
 
 
 def per_device(
@@ -362,11 +371,13 @@
     leaf_basis, local_trans, local_coupling, up_trans, coupling,
 ):
     hbm = pl.BlockSpec(memory_space=pltpu.HBM)
-    smem = pl.BlockSpec(memory_space=pltpu.SMEM)
     nlocal = 2 * LEAVES - 2
     npeers = sum((1 << n) - 1 for _, n in PHASES)
     vm = pltpu.VMEM
     scratch = [
+        vm((RHS, SPAN), f32),
+        pltpu.SMEM((NNEAR, LEAVES), jnp.int32),
+        pltpu.SMEM((LEAVES,), jnp.int32),
         vm((RHS, SPAN), f32),
         vm((3, SPAN), f32),
         vm((1, SPAN), f32),
@@ -399,7 +410,8 @@
         vm((RANK, 9 * RANK), bf16),
         vm((LEVELS, RHS, 2 * RANK), f32),
         vm((npeers, RHS, 2 * RANK), f32),
-        pltpu.SemaphoreType.DMA((8,)),
+        pltpu.SemaphoreType.DMA((10,)),
+        pltpu.SemaphoreType.DMA((4,)),
         pltpu.SemaphoreType.DMA((npeers,)),
         pltpu.SemaphoreType.DMA((npeers,)),
         pltpu.SemaphoreType.DMA((2,)),
@@ -408,14 +420,14 @@
     return pl.pallas_call(
         kernel,
         out_shape=jax.ShapeDtypeStruct((RHS, SPAN), f32),
-        in_specs=[hbm, hbm, hbm, smem, smem, hbm, hbm, hbm, hbm, hbm],
-        out_specs=pl.BlockSpec(memory_space=pltpu.VMEM),
+        in_specs=[hbm] * 10,
+        out_specs=hbm,
         scratch_shapes=scratch,
         compiler_params=pltpu.CompilerParams(
-            collective_id=0, has_side_effects=True, vmem_limit_bytes=40 * 1024 * 1024
+            collective_id=0, has_side_effects=True, vmem_limit_bytes=63 * 1024 * 1024
         ),
     )(
-        densities, panels, areas.reshape(1, SPAN), near_offsets, near_count,
+        densities, panels, areas.reshape(1, SPAN), near_offsets.T, near_count,
         leaf_basis, local_trans, local_coupling, up_trans, coupling,
     )
 

time: 42 us -> 25 us (0.60)
  local copies, waits for them, and re-layouts: 10.7 us -> 1.57 us
  Pallas kernels: 30.9 us -> 23.1 us
    unnamed x20 -> x1, local copies, waits for them, and re-layouts: 10.7 us -> 1.57 us
    pallas_call x1, Pallas kernels: 30.9 us -> 23.1 us  [per_device(): pl.pallas_call(kernel, out_shape=jax.ShapeDtypeStruct((RHS, SPAN), f32),...]
where the time goes in v2:
time: 25 us; the launch traced here: 24.6 us
  Pallas kernels  23.1 us (92%)
  local copies, waits for them, and re-layouts  1.57 us (6%)
    pallas_call x1, Pallas kernels, per_device(): pl.pallas_call(kernel, out_shape=jax.ShapeDtypeStruct((RHS, SPAN), f32),...  23.1 us
    unnamed x1, local copies, waits for them, and re-layouts  1.57 us

profile of v2, /device:TPU:1, one launch (start us, length us, event | category | flops | bytes accessed | tf_op | source)
XLA Modules:
  0.0 24.6 jit_solution(8443125575209353087)
XLA Ops:
  0.0 23.1 %shard_map.100 = f32[16,2048]{1,0:T(8,128)} custom-call(f32[16,2048]{1,0:T(8,128)} %dens_hbm.1, f32[3,2048]{1,0:T(4,128)} %pan_hbm.1, f32[1,2048]{1,0:T(1,128)} %bitcast.2, s32[6,32]{1,0:T(8,128)} %bitcast.3, s32[32]{0:T(128)} %cnt_hbm.1, f32[32,64,64]{2,1,0:T(8,128)} %bas_hbm.1, f32[62,64,64]{2,1,0:T(8,128)} %ltr_hbm.1, f32[62,64,64]{2,1,0:T(8,128)} %lco_hbm.1, ...), custom_call_target="tpu_custom_call" | custom-call | tf_op jit(solution)/shard_map/pallas_call | solution.py:420
  23.1 1.6 %copy.12 = f32[16,2048]{1,0:T(8,128)} copy(f32[16,2048]{1,0:T(8,128)} %shard_map.100) | data formatting | bytes 262144

commit v3 on v2

--- a/solution.py
+++ b/solution.py
@@ -15,6 +15,7 @@
 DEPTH = 5
 NODES = 256
 SPAN = LEAVES * LEAF
+NOLEAF = LEAVES + 2 * HALO
 softening = 0.25
 MESH = pl.DeviceIdType.MESH
 f32 = jnp.float32
@@ -23,6 +24,13 @@
 PHASES = ((0, 3), (3, 2), (5, 3))
 START = [2 * LEAVES - 2 * (LEAVES >> j) for j in range(DEPTH)]
 PAIR = [s // 2 for s in START]
+
+
+def hops(p):
+    count = 0
+    for bits, size in ((p >> 1 & 3, 4), (p >> 3 & 3, 4), (p >> 5, 8)):
+        count += max(min((a ^ bits) - a & size - 1, a - (a ^ bits) & size - 1) for a in range(size))
+    return count
 
 
 def split(x):
@@ -68,12 +76,12 @@
 
 def kernel(
     dens_hbm, pan_hbm, area_hbm, off_hbm, cnt_hbm, bas_hbm, ltr_hbm, lco_hbm, upt_hbm, cpl_hbm,
-    out_hbm,
-    out_ref, off_ref, cnt_ref, dens, pan, area, bas, ltr, lco, upt, cpl,
+    out_ref,
+    off_ref, cnt_ref, dens, pan, area, bas, ltr, lco, upt, cpl,
     bas_h, bas_l, ltr_h, ltr_l, gch, gcl, dh, dl,
-    blocks, points, qrow, gpair, hpair, acc,
+    coords, charge, ends, halo, column, points, qrow, gpair, hpair, acc,
     wt1h, wt1l, wt2h, wt2l, wt3h, wt3l, wk_h, wk_l,
-    send, recv, load_sem, store_sem, send_sem, recv_sem, halo_ssem, halo_rsem,
+    send, recv, load_sem, send_sem, recv_sem, halo_ssem, halo_rsem,
 ):
     me = lax.axis_index("leaf")
     right = lax.rem(me + 1, NODES)
@@ -160,7 +168,7 @@
         for k in range(levels):
             send[slot + k] = messages[k]
         copies = []
-        for p in reversed(range(1, 1 << levels)):
+        for p in sorted(range(1, 1 << levels), key=lambda p: -hops(p << first)):
             copy = pltpu.make_async_remote_copy(
                 src_ref=send.at[slot + p.bit_length() - 1],
                 dst_ref=recv.at[base + p - 1],
@@ -195,22 +203,28 @@
     loads["area"].wait()
     halo_rows = jnp.zeros((5, 2 * LEAF), f32)
 
+    def place(tile, slot):
+        coords[slot] = tile[RHS:]
+        coords[slot + 1] = pltpu.roll(tile[RHS:], LEAF, 1)
+        high, rest = split(tile[:RHS].T)
+        charge[pl.ds(slot, 2)] = jnp.concatenate([high, rest], 1).reshape(2, LEAF, 2 * RHS)
+
     def pack(p):
         at = rows_at(p, 2 * LEAF)
-        coords = jnp.concatenate([pan[:, at], halo_rows], 0)
-        tile = jnp.concatenate([dens[:, at] * area[:, at], coords], 0)
-        blocks[HALO + 2 * p] = tile
-        blocks[HALO + 2 * p + 1] = pltpu.roll(tile, LEAF, 1)
-        points[at, :] = coords.T
-
-    sweep(LEAVES // 2, pack, 16)
+        where = jnp.concatenate([pan[:, at], halo_rows], 0)
+        tile = jnp.concatenate([dens[:, at] * area[:, at], where], 0)
+        if p in (0, 1, 14, 15):
+            ends[p if p < 2 else p - 12] = tile
+        place(tile, HALO + 2 * p)
+        points[at, :] = where.T
+
+    for p in (0, 1, 14, 15):
+        pack(p)
     halos = []
-    for at, (source, target, device) in enumerate(
-        ((LEAVES, 0, right), (HALO, HALO + LEAVES, left))
-    ):
+    for at, (source, target, device) in enumerate(((2, 0, right), (0, 2, left))):
         copy = pltpu.make_async_remote_copy(
-            src_ref=blocks.at[pl.ds(source, HALO)],
-            dst_ref=blocks.at[pl.ds(target, HALO)],
+            src_ref=ends.at[pl.ds(source, 2)],
+            dst_ref=halo.at[pl.ds(target, 2)],
             send_sem=halo_ssem.at[at],
             recv_sem=halo_rsem.at[at],
             device_id=(device,),
@@ -218,6 +232,11 @@
         )
         copy.start()
         halos.append(copy)
+    for p in range(2, 14):
+        pack(p)
+    coords[NOLEAF] = jnp.zeros((8, 2 * LEAF), f32)
+    coords[NOLEAF + 1] = jnp.zeros((8, 2 * LEAF), f32)
+    charge[NOLEAF] = jnp.zeros((LEAF, 2 * RHS), bf16)
 
     u4, u5 = chain(3, 2)
     wt2h[...], wt2l[...] = split(jnp.concatenate([u5, zero, u5, u4], 1))
@@ -284,37 +303,42 @@
     loads["cnt"].wait()
     for copy in halos:
         copy.wait()
-    for target, edge in ((0, 0), (HALO + LEAVES, NODES - 1)):
+    for end, slot, edge in ((0, 0, 0), (2, HALO + LEAVES, NODES - 1)):
         keep = jnp.where(me == edge, 0.0, 1.0)
-        for j in range(target, target + HALO):
-            blocks[j] = blocks[j] * keep
+        for t in range(2):
+            place(halo[end + t] * keep, slot + 2 * t)
 
     def near_leaf(i):
         at = rows_at(i, LEAF)
-        tx, ty, tz = (points[at, c : c + 1] for c in range(3))
+        tx, ty, tz = (jnp.broadcast_to(points[at, c : c + 1], (LEAF, 2 * LEAF)) for c in range(3))
         count = cnt_ref[i]
         kernels, charges = [], []
         for t in range(NNEAR // 2):
-            j0 = off_ref[2 * t, i] + (i + HALO)
-            j1 = off_ref[2 * t + 1, i] + (i + HALO)
-            c = jnp.where(low, blocks[j0], blocks[j1 ^ 1])
-            live = jnp.where(low, 2 * t, 2 * t + 1) < count
-            charges.append(jnp.where(live, c[:RHS], 0.0))
-            dx = tx - c[RHS : RHS + 1]
-            dy = ty - c[RHS + 1 : RHS + 2]
-            dz = tz - c[RHS + 2 : RHS + 3]
-            kernels.append(lax.rsqrt(dx * dx + dy * dy + dz * dz + softening))
-        return product(
-            split(jnp.concatenate(charges, 1)), split(jnp.concatenate(kernels, 1)), dot_t
-        )
+            j = [
+                jnp.where(s < count, off_ref[s, i] + (i + HALO), NOLEAF)
+                for s in (2 * t, 2 * t + 1)
+            ]
+            charges += [charge[j[0]], charge[j[1]]]
+            c = jnp.where(low, coords[j[0]], coords[j[1] ^ 1])
+            dx = tx - c[0:1]
+            dy = ty - c[1:2]
+            dz = tz - c[2:3]
+            kernels.append(lax.rsqrt(dx * dx + dy * dy + (dz * dz + softening)))
+        high, rest = split(jnp.concatenate(kernels, 1))
+        both = dot(jnp.concatenate([high, rest], 0), jnp.concatenate(charges, 0))
+        column[at, :] = both[:LEAF] + both[LEAF:]
 
     def near(p):
-        tile = jnp.concatenate([near_leaf(2 * p), near_leaf(2 * p + 1)], 1)
+        near_leaf(2 * p)
+        near_leaf(2 * p + 1)
+
+    def near_fold(p):
         at = rows_at(p, 2 * LEAF)
-        acc[:, at] = acc[:, at] + tile
+        tile = column[at, :].T
+        acc[:, at] = acc[:, at] + (tile[:RHS] + tile[RHS:])
 
     def near_some(first, last):
-        lax.fori_loop(first // 2, last // 2, lambda p, carry: (near(2 * p), near(2 * p + 1), carry)[2], 0)
+        sweep(last - first, lambda p: near(p + first), 4)
 
     near_some(0, 8)
 
@@ -351,19 +375,16 @@
 
     sweep(LEAVES, compose_leaf, 16)
     near_some(8, 16)
+    for p in range(LEAVES // 2):
+        near_fold(p)
 
     s5, s6, s7 = receive()
     tail = split(jnp.concatenate([s5 + s6, s7], 1))
     w = (wk_h[:, 5 * RANK :], wk_l[:, 5 * RANK :])
     local = split(local + product(tail, w, dot_t))
-    stores = []
     for b in range(4):
         at = rows_at(b, 512)
         out_ref[:, at] = acc[:, at] + product(local, (dh[at], dl[at]), dot_t)
-        stores.append(pltpu.make_async_copy(out_ref.at[:, at], out_hbm.at[:, at], store_sem.at[b]))
-        stores[-1].start()
-    for copy in stores:
-        copy.wait()
 
 
 def per_device(
@@ -375,7 +396,6 @@
     npeers = sum((1 << n) - 1 for _, n in PHASES)
     vm = pltpu.VMEM
     scratch = [
-        vm((RHS, SPAN), f32),
         pltpu.SMEM((NNEAR, LEAVES), jnp.int32),
         pltpu.SMEM((LEAVES,), jnp.int32),
         vm((RHS, SPAN), f32),
@@ -394,7 +414,11 @@
         vm((nlocal * RANK, RANK), bf16),
         vm((SPAN, RANK), bf16),
         vm((SPAN, RANK), bf16),
-        vm((LEAVES + 2 * HALO, 24, 2 * LEAF), f32),
+        vm((NOLEAF + 2, 8, 2 * LEAF), f32),
+        vm((NOLEAF + 1, LEAF, 2 * RHS), bf16),
+        vm((4, RHS + 8, 2 * LEAF), f32),
+        vm((4, RHS + 8, 2 * LEAF), f32),
+        vm((SPAN, 2 * RHS), f32),
         vm((SPAN, 8), f32),
         vm((nlocal // 2, 2 * RHS, RANK), f32),
         vm((nlocal // 2, RHS, 2 * RANK), f32),
@@ -411,7 +435,6 @@
         vm((LEVELS, RHS, 2 * RANK), f32),
         vm((npeers, RHS, 2 * RANK), f32),
         pltpu.SemaphoreType.DMA((10,)),
-        pltpu.SemaphoreType.DMA((4,)),
         pltpu.SemaphoreType.DMA((npeers,)),
         pltpu.SemaphoreType.DMA((npeers,)),
         pltpu.SemaphoreType.DMA((2,)),
@@ -421,15 +444,16 @@
         kernel,
         out_shape=jax.ShapeDtypeStruct((RHS, SPAN), f32),
         in_specs=[hbm] * 10,
-        out_specs=hbm,
+        out_specs=pl.BlockSpec(memory_space=pltpu.VMEM),
         scratch_shapes=scratch,
         compiler_params=pltpu.CompilerParams(
-            collective_id=0, has_side_effects=True, vmem_limit_bytes=63 * 1024 * 1024
+            collective_id=0, has_side_effects=True, vmem_limit_bytes=40 * 1024 * 1024
         ),
-    )(
-        densities, panels, areas.reshape(1, SPAN), near_offsets.T, near_count,
-        leaf_basis, local_trans, local_coupling, up_trans, coupling,
-    )
+    )(*[
+        pltpu.with_memory_space_constraint(v, pltpu.HBM)
+        for v in (densities, panels, areas.reshape(1, SPAN), near_offsets.T, near_count,
+        leaf_basis, local_trans, local_coupling, up_trans, coupling)
+    ])
 
 
 def solution(mesh):

time: 25 us -> 23.2 us (0.928); the launches traced: 24.6 us -> 23.1 us
  local copies, waits for them, and re-layouts: 1.57 us -> 0.66 us
  Pallas kernels: 23.1 us -> 22.4 us
    unnamed x1, local copies, waits for them, and re-layouts: 1.57 us -> 0.66 us
    pallas_call x1, Pallas kernels: 23.1 us -> 22.4 us  [per_device(): pl.pallas_call(kernel, out_shape=jax.ShapeDtypeStruct((RHS, SPAN), f32),...]
where the time goes in v3:
time: 23.2 us; the launch traced here: 23.1 us
  Pallas kernels  22.4 us (97%)
  local copies, waits for them, and re-layouts  0.66 us (3%)
    pallas_call x1, Pallas kernels, per_device(): pl.pallas_call(kernel, out_shape=jax.ShapeDtypeStruct((RHS, SPAN), f32),...  22.4 us
    unnamed x1, local copies, waits for them, and re-layouts  0.66 us

profile of v3, /device:TPU:1, one launch (start us, length us, event | category | flops | bytes accessed | tf_op | source)
XLA Modules:
  0.0 23.1 jit_solution(12487181498504544777)
XLA Ops:
  0.0 22.4 %shard_map.100 = f32[16,2048]{1,0:T(8,128)S(1)} custom-call(f32[16,2048]{1,0:T(8,128)} %dens_hbm.1, f32[3,2048]{1,0:T(4,128)} %pan_hbm.1, f32[1,2048]{1,0:T(1,128)} %bitcast.2, s32[6,32]{1,0:T(8,128)} %bitcast.3, s32[32]{0:T(128)} %cnt_hbm.1, f32[32,64,64]{2,1,0:T(8,128)} %bas_hbm.1, f32[62,64,64]{2,1,0:T(8,128)} %ltr_hbm.1, f32[62,64,64]{2,1,0:T(8,128)} %lco_hbm.1, ...), custom_call_target="tpu_custom_call" | custom-call | tf_op jit(solution)/shard_map/pallas_call | solution.py:443
  22.4 0.7 %copy.12 = f32[16,2048]{1,0:T(8,128)} copy(f32[16,2048]{1,0:T(8,128)S(1)} %shard_map.100) | data formatting | bytes 262144

commit v4 on v3

--- a/solution.py
+++ b/solution.py
@@ -78,7 +78,7 @@
     dens_hbm, pan_hbm, area_hbm, off_hbm, cnt_hbm, bas_hbm, ltr_hbm, lco_hbm, upt_hbm, cpl_hbm,
     out_ref,
     off_ref, cnt_ref, dens, pan, area, bas, ltr, lco, upt, cpl,
-    bas_h, bas_l, ltr_h, ltr_l, gch, gcl, dh, dl,
+    bas_h, bas_l, ltr_h, ltr_l, gch, gcl, dt,
     coords, charge, ends, halo, column, points, qrow, gpair, hpair, acc,
     wt1h, wt1l, wt2h, wt2l, wt3h, wt3l, wk_h, wk_l,
     send, recv, load_sem, send_sem, recv_sem, halo_ssem, halo_rsem,
@@ -247,12 +247,12 @@
     t5 = product(split(t3), split(u5), dot)
     t6 = product(split(t5), e[5], dot)
     t7 = product(split(t5), split(v7), dot)
-    blank = jnp.zeros((RANK, RANK), bf16)
+    blank = jnp.zeros((2 * RANK, RANK), bf16)
     wk_h[:, rows_at(LEVELS, RANK)] = blank
     wk_l[:, rows_at(LEVELS, RANK)] = blank
     for k, t in enumerate((None, t1, t2, t3, t4, t5, t6, t7)):
         w = cpl[0, k] if t is None else product(split(t), split(cpl[0, k]), dot)
-        wk_h[:, rows_at(k, RANK)], wk_l[:, rows_at(k, RANK)] = split(w)
+        wk_h[:, rows_at(k, RANK)], wk_l[:, rows_at(k, RANK)] = split(jnp.concatenate([w, w], 0))
 
     loads["lco"].wait()
 
@@ -350,7 +350,7 @@
     own = [jnp.concatenate([coef, half], 1), own[:, : 2 * RANK], own[:, 2 * RANK :]]
     receive = exchange(2, own)
 
-    local = half
+    local = jnp.zeros((RHS, 2 * RANK), f32)
     for k in range(5):
         w = (wk_h[:, rows_at(k, RANK)], wk_l[:, rows_at(k, RANK)])
         local = local + product(split(early[k]), w, dot_t)
@@ -369,11 +369,15 @@
 
         sweep(LEAVES >> (level + 1), compose, 16)
 
-    def compose_leaf(i):
-        at = rows_at(i, LEAF)
-        dh[at], dl[at] = split(product((bas_h[at], bas_l[at]), (gch[at], gcl[at]), dot))
-
-    sweep(LEAVES, compose_leaf, 16)
+    def compose_leaf(p):
+        pair = []
+        for i in (2 * p, 2 * p + 1):
+            at = rows_at(i, LEAF)
+            pair.append(product((bas_h[at], bas_l[at]), (gch[at], gcl[at]), dot))
+        high, rest = split(jnp.concatenate(pair, 0).T)
+        dt[:, rows_at(p, 2 * LEAF)] = jnp.concatenate([high, rest], 0)
+
+    sweep(LEAVES // 2, compose_leaf, 8)
     near_some(8, 16)
     for p in range(LEAVES // 2):
         near_fold(p)
@@ -381,10 +385,13 @@
     s5, s6, s7 = receive()
     tail = split(jnp.concatenate([s5 + s6, s7], 1))
     w = (wk_h[:, 5 * RANK :], wk_l[:, 5 * RANK :])
-    local = split(local + product(tail, w, dot_t))
+    high, rest = split(local + product(tail, w, dot_t))
+    rest = jnp.where(low, rest.astype(f32), 0.0).astype(bf16)
+    local = jnp.concatenate([high, rest], 0)
     for b in range(4):
         at = rows_at(b, 512)
-        out_ref[:, at] = acc[:, at] + product(local, (dh[at], dl[at]), dot_t)
+        far = dot(local, dt[:, at])
+        out_ref[:, at] = acc[:, at] + (far[:RHS] + far[RHS:])
 
 
 def per_device(
@@ -412,8 +419,7 @@
         vm((nlocal * RANK, RANK), bf16),
         vm((nlocal * RANK, RANK), bf16),
         vm((nlocal * RANK, RANK), bf16),
-        vm((SPAN, RANK), bf16),
-        vm((SPAN, RANK), bf16),
+        vm((2 * RANK, SPAN), bf16),
         vm((NOLEAF + 2, 8, 2 * LEAF), f32),
         vm((NOLEAF + 1, LEAF, 2 * RHS), bf16),
         vm((4, RHS + 8, 2 * LEAF), f32),
@@ -430,8 +436,8 @@
         vm((RANK, 4 * RANK), bf16),
         vm((RANK, 4 * RANK), bf16),
         vm((RANK, 4 * RANK), bf16),
-        vm((RANK, 9 * RANK), bf16),
-        vm((RANK, 9 * RANK), bf16),
+        vm((2 * RANK, 9 * RANK), bf16),
+        vm((2 * RANK, 9 * RANK), bf16),
         vm((LEVELS, RHS, 2 * RANK), f32),
         vm((npeers, RHS, 2 * RANK), f32),
         pltpu.SemaphoreType.DMA((10,)),

time: 23.2 us -> 23 us (level)
  no operation moved by 1% of the time
where the time goes in v4:
time: 23 us; the launch traced here: 22.9 us
  Pallas kernels  22.3 us (97%)
  local copies, waits for them, and re-layouts  0.66 us (3%)
    pallas_call x1, Pallas kernels, per_device(): pl.pallas_call(kernel, out_shape=jax.ShapeDtypeStruct((RHS, SPAN), f32),...  22.3 us
    unnamed x1, local copies, waits for them, and re-layouts  0.66 us

profile of v4, /device:TPU:1, one launch (start us, length us, event | category | flops | bytes accessed | tf_op | source)
XLA Modules:
  0.0 22.9 jit_solution(5635080552569136587)
XLA Ops:
  0.0 22.3 %shard_map.100 = f32[16,2048]{1,0:T(8,128)S(1)} custom-call(f32[16,2048]{1,0:T(8,128)} %dens_hbm.1, f32[3,2048]{1,0:T(4,128)} %pan_hbm.1, f32[1,2048]{1,0:T(1,128)} %bitcast.2, s32[6,32]{1,0:T(8,128)} %bitcast.3, s32[32]{0:T(128)} %cnt_hbm.1, f32[32,64,64]{2,1,0:T(8,128)} %bas_hbm.1, f32[62,64,64]{2,1,0:T(8,128)} %ltr_hbm.1, f32[62,64,64]{2,1,0:T(8,128)} %lco_hbm.1, ...), custom_call_target="tpu_custom_call" | custom-call | tf_op jit(solution)/shard_map/pallas_call | solution.py:449
  22.3 0.7 %copy.12 = f32[16,2048]{1,0:T(8,128)} copy(f32[16,2048]{1,0:T(8,128)S(1)} %shard_map.100) | data formatting | bytes 262144

commit v5 on v4

--- a/solution.py
+++ b/solution.py
@@ -91,7 +91,8 @@
         (
             ("dens", dens_hbm, dens),
             ("bas", bas_hbm, bas),
-            ("ltr", ltr_hbm, ltr),
+            ("ltr", ltr_hbm.at[pl.ds(0, 32)], ltr.at[pl.ds(0, 32)]),
+            ("ltu", ltr_hbm.at[pl.ds(32, 30)], ltr.at[pl.ds(32, 30)]),
             ("upt", upt_hbm, upt),
             ("pan", pan_hbm, pan),
             ("area", area_hbm, area),
@@ -139,6 +140,8 @@
         return product(split(q), w, dot)
 
     for level in range(DEPTH - 1):
+        if level == 1:
+            loads["ltu"].wait()
 
         def lift_two(m, level=level):
             qrow[PAIR[level + 1] + m] = jnp.concatenate(
@@ -160,6 +163,8 @@
     t1, t2, t3 = chain(0, 3)
     wt1h[...], wt1l[...] = split(jnp.concatenate([t3, zero, t3, t1, t3, t2], 1))
     coef = lift(DEPTH - 1, 0)
+
+    pending = []
 
     def exchange(phase, messages):
         first, levels = PHASES[phase]
@@ -182,7 +187,8 @@
 
         def receive():
             for copy in copies:
-                copy.wait()
+                copy.wait_recv()
+            pending.extend(copies)
             sums = []
             for k in range(levels):
                 parts = [recv[base + p - 1] for p in range(1 << k, 2 << k)]
@@ -385,6 +391,8 @@
     s5, s6, s7 = receive()
     tail = split(jnp.concatenate([s5 + s6, s7], 1))
     w = (wk_h[:, 5 * RANK :], wk_l[:, 5 * RANK :])
+    for copy in pending:
+        copy.wait_send()
     high, rest = split(local + product(tail, w, dot_t))
     rest = jnp.where(low, rest.astype(f32), 0.0).astype(bf16)
     local = jnp.concatenate([high, rest], 0)
@@ -440,7 +448,7 @@
         vm((2 * RANK, 9 * RANK), bf16),
         vm((LEVELS, RHS, 2 * RANK), f32),
         vm((npeers, RHS, 2 * RANK), f32),
-        pltpu.SemaphoreType.DMA((10,)),
+        pltpu.SemaphoreType.DMA((11,)),
         pltpu.SemaphoreType.DMA((npeers,)),
         pltpu.SemaphoreType.DMA((npeers,)),
         pltpu.SemaphoreType.DMA((2,)),

time: 23 us -> 22.9 us (level)
  no operation moved by 1% of the time
where the time goes in v5:
time: 22.9 us; the launch traced here: 22.8 us
  Pallas kernels  22.2 us (97%)
  local copies, waits for them, and re-layouts  0.66 us (3%)
    pallas_call x1, Pallas kernels, per_device(): pl.pallas_call(kernel, out_shape=jax.ShapeDtypeStruct((RHS, SPAN), f32),...  22.2 us
    unnamed x1, local copies, waits for them, and re-layouts  0.66 us

profile of v5, /device:TPU:1, one launch (start us, length us, event | category | flops | bytes accessed | tf_op | source)
XLA Modules:
  0.0 22.8 jit_solution(14649437503749617960)
XLA Ops:
  0.0 22.2 %shard_map.100 = f32[16,2048]{1,0:T(8,128)S(1)} custom-call(f32[16,2048]{1,0:T(8,128)} %dens_hbm.1, f32[3,2048]{1,0:T(4,128)} %pan_hbm.1, f32[1,2048]{1,0:T(1,128)} %bitcast.2, s32[6,32]{1,0:T(8,128)} %bitcast.3, s32[32]{0:T(128)} %cnt_hbm.1, f32[32,64,64]{2,1,0:T(8,128)} %bas_hbm.1, f32[62,64,64]{2,1,0:T(8,128)} %ltr_hbm.1, f32[62,64,64]{2,1,0:T(8,128)} %lco_hbm.1, ...), custom_call_target="tpu_custom_call" | custom-call | tf_op jit(solution)/shard_map/pallas_call | solution.py:457
  22.2 0.7 %copy.12 = f32[16,2048]{1,0:T(8,128)} copy(f32[16,2048]{1,0:T(8,128)S(1)} %shard_map.100) | data formatting | bytes 262144

commit v6 on v5

--- a/solution.py
+++ b/solution.py
@@ -273,6 +273,20 @@
     for p in range(28, 31):
         couple(p)
 
+    top = rows_at(PAIR[4], 2 * RANK)
+    gch[top] = ltr_h[top]
+    gcl[top] = ltr_l[top]
+    for level in range(DEPTH - 2, -1, -1):
+
+        def compose(m, level=level):
+            at = rows_at(PAIR[level] + m, 2 * RANK)
+            up = rows_at(START[level + 1] + m, RANK)
+            gch[at], gcl[at] = split(
+                product((ltr_h[at], ltr_l[at]), (gch[up], gcl[up]), dot)
+            )
+
+        sweep(LEAVES >> (level + 1), compose, 16)
+
     sums = receive()
     tot = own[0] + (sums[0] + (sums[1] + sums[2]))
     coef = tot[:, :RANK]
@@ -360,20 +374,6 @@
     for k in range(5):
         w = (wk_h[:, rows_at(k, RANK)], wk_l[:, rows_at(k, RANK)])
         local = local + product(split(early[k]), w, dot_t)
-
-    top = rows_at(PAIR[4], 2 * RANK)
-    gch[top] = ltr_h[top]
-    gcl[top] = ltr_l[top]
-    for level in range(DEPTH - 2, -1, -1):
-
-        def compose(m, level=level):
-            at = rows_at(PAIR[level] + m, 2 * RANK)
-            up = rows_at(START[level + 1] + m, RANK)
-            gch[at], gcl[at] = split(
-                product((ltr_h[at], ltr_l[at]), (gch[up], gcl[up]), dot)
-            )
-
-        sweep(LEAVES >> (level + 1), compose, 16)
 
     def compose_leaf(p):
         pair = []

time: 22.9 us -> 22.9 us (level)
  no operation moved by 1% of the time
where the time goes in v6:
time: 22.9 us; the launch traced here: 22.8 us
  Pallas kernels  22.2 us (97%)
  local copies, waits for them, and re-layouts  0.66 us (3%)
    pallas_call x1, Pallas kernels, per_device(): pl.pallas_call(kernel, out_shape=jax.ShapeDtypeStruct((RHS, SPAN), f32),...  22.2 us
    unnamed x1, local copies, waits for them, and re-layouts  0.66 us

profile of v6, /device:TPU:1, one launch (start us, length us, event | category | flops | bytes accessed | tf_op | source)
XLA Modules:
  0.0 22.8 jit_solution(11473564229123011084)
XLA Ops:
  0.0 22.2 %shard_map.100 = f32[16,2048]{1,0:T(8,128)S(1)} custom-call(f32[16,2048]{1,0:T(8,128)} %dens_hbm.1, f32[3,2048]{1,0:T(4,128)} %pan_hbm.1, f32[1,2048]{1,0:T(1,128)} %bitcast.2, s32[6,32]{1,0:T(8,128)} %bitcast.3, s32[32]{0:T(128)} %cnt_hbm.1, f32[32,64,64]{2,1,0:T(8,128)} %bas_hbm.1, f32[62,64,64]{2,1,0:T(8,128)} %ltr_hbm.1, f32[62,64,64]{2,1,0:T(8,128)} %lco_hbm.1, ...), custom_call_target="tpu_custom_call" | custom-call | tf_op jit(solution)/shard_map/pallas_call | solution.py:457
  22.2 0.7 %copy.12 = f32[16,2048]{1,0:T(8,128)} copy(f32[16,2048]{1,0:T(8,128)S(1)} %shard_map.100) | data formatting | bytes 262144
